TPU v7x, 128 devices: a whole 4x4x4 slice. The times are simulated.
128 devices in a mesh: col: 32 (over x, y, core), row: 4 (over z).
Axes of the slice: x: 4, y: 4, z: 4, core: 2. Of those that a mesh axis runs over, the one named last changes fastest.
Arguments:
- rhs: float32 [2, 32, 4, 4096], P(None, None, 'row', 'col'), may hold values from -6 to 6
- u_factor: bfloat16 [64, 160, 2, 256, 128], P('row', 'col'), may hold values from -0.0390625 to 0.0390625
- v_factor: bfloat16 [64, 160, 2, 256, 128], P('row', 'col'), may hold values from -0.375 to 0.375
- ranks: int32 [64, 160], P('row', 'col'), may hold values from 8 to 128, as said below
- assign: int32 [160], replicated, may hold values from 0 to 159, each once
Outputs:
- solution: float32 [2, 32, 40960], P(None, None, 'col')
- residual_estimate: float32 [32], replicated
Inputs may be any that keep to these rules, and one draw needn't show every extreme that they name: `ranks`: every entry is 128 // 16 times a power of two from 1 to 16.
All inputs are finite; a program needn't handle non-finite values.
Results may differ from a plain program's by a relative error of at most 0.0068.
Values may be sent and summed in bfloat16 or wider, within the bound.
A program may use at most 128 MiB of HBM per device.

v0:
```python
import jax
import jax.numpy as jnp
from jax import lax
from jax.sharding import Mesh
from jax.sharding import PartitionSpec as P

ITERS = 2
COL = ("col_0", "col_1", "col_2")
COL_ROW = ("col_0", "col_1", "col_2", "row")


def cut_along(x, dim, devices):
    before, after = (x.shape[:dim], x.shape[dim + 1 :])
    return jnp.moveaxis(x.reshape(*before, devices, -1, *after), dim, 0)


def sent_and_summed(x, axis, dim):
    devices = lax.axis_size(axis)
    tiles = lax.all_to_all(cut_along(x, dim, devices), axis, 0, 0, tiled=True)
    return jnp.sum(tiles.astype(jnp.float32), axis=0)


def in_order(tiles, dim):
    tiles = jnp.moveaxis(tiles, 0, dim)
    dims = tiles.shape
    return tiles.reshape(*dims[:dim], dims[dim] * dims[dim + 1], *dims[dim + 2 :])


def copy_for_each(x, axis):
    copies = jnp.broadcast_to(x, (lax.axis_size(axis), *x.shape))
    return lax.all_to_all(copies, axis, split_axis=0, concat_axis=0, tiled=True)


def collect(x, axis, dim):
    return in_order(copy_for_each(x, axis), dim)


def by_axis(x, axes):
    for axis in axes:
        x = lax.psum(x, axis)
    return x


def over_copies(x, axis):
    everything = copy_for_each(x, axis)
    return jnp.sum(everything.astype(jnp.float32), axis=0)


def over_copies_2(x, axis):
    everything = copy_for_each(x, axis)
    return jnp.sum(everything, axis=0)


def sum_squares(value):
    return jnp.sum(value * value, axis=(0, 2))


def on_device(rhs, u_factor, v_factor, ranks, assign):
    tile_rows = u_factor.shape[0]
    tile_cols = u_factor.shape[1]
    tile_size = u_factor.shape[3]
    rank_cap = u_factor.shape[4]
    sources = rhs.shape[1]
    rank_iota = lax.broadcasted_iota(jnp.int32, (tile_rows, tile_cols, 1, 1, rank_cap), 4)
    mask = (rank_iota < ranks[:, :, None, None, None]).astype(jnp.float32)

    def adjoint_terms(group_data):
        data_b = group_data.reshape(2, sources, tile_rows, tile_size)
        raw = jnp.einsum("ipcnk,dsin->ipcdsk", u_factor, data_b, preferred_element_type=jnp.float32)
        coeff = jnp.stack(
            [raw[:, :, 0, 0] + raw[:, :, 1, 1], raw[:, :, 0, 1] - raw[:, :, 1, 0]], axis=2
        )
        coeff = (coeff * mask).astype(jnp.bfloat16)
        prod = jnp.einsum("ipcnk,ipdsk->cdspn", v_factor, coeff, preferred_element_type=jnp.float32)
        partial_model = jnp.stack([prod[0, 0] + prod[1, 1], prod[0, 1] - prod[1, 0]], axis=0)
        return partial_model.reshape(2, sources, tile_cols * tile_size)

    def adjoint_step(data_hat, v_prev):
        group_data = collect(data_hat.astype(jnp.bfloat16), COL, 2)
        beta_now = jnp.sqrt(by_axis(sum_squares(data_hat), COL_ROW))
        model_sum = over_copies(adjoint_terms(group_data).astype(jnp.bfloat16), "row").astype(
            jnp.float32
        )
        v_hat = model_sum / beta_now[None, :, None] - beta_now[None, :, None] * v_prev
        alpha_now = jnp.sqrt(over_copies_2(sum_squares(v_hat), COL))
        return (
            data_hat / beta_now[None, :, None],
            beta_now,
            v_hat / alpha_now[None, :, None],
            alpha_now,
        )

    data_first = rhs.reshape(2, sources, rhs.shape[3])
    zero_model = jnp.zeros((2, sources, tile_cols * tile_size), jnp.float32)
    u_vec, beta_now, v_vec, alpha_now = adjoint_step(data_first, zero_model)
    w_vec = v_vec
    x_vec = zero_model
    phibar = beta_now
    rhobar = alpha_now
    for iteration in range(ITERS):
        model_b = v_vec.astype(jnp.bfloat16).reshape(2, sources, tile_cols, tile_size)
        forward_raw = jnp.einsum(
            "ipcnk,dspn->ipcdsk", v_factor, model_b, preferred_element_type=jnp.float32
        )
        forward_coeff = jnp.stack(
            [
                forward_raw[:, :, 0, 0] - forward_raw[:, :, 1, 1],
                forward_raw[:, :, 0, 1] + forward_raw[:, :, 1, 0],
            ],
            axis=2,
        )
        forward_coeff = (forward_coeff * mask).astype(jnp.bfloat16)
        forward_prod = jnp.einsum(
            "ipcnk,ipdsk->cdsin", u_factor, forward_coeff, preferred_element_type=jnp.float32
        )
        partial_data = jnp.stack(
            [forward_prod[0, 0] - forward_prod[1, 1], forward_prod[0, 1] + forward_prod[1, 0]],
            axis=0,
        )
        partial_data = partial_data.reshape(2, sources, tile_rows * tile_size)
        data_hat = (
            sent_and_summed(partial_data.astype(jnp.bfloat16), COL, 2)
            - alpha_now[None, :, None] * u_vec
        )
        u_vec, beta_now, v_vec, alpha_now = adjoint_step(data_hat, v_vec)
        rho_now = jnp.sqrt(rhobar * rhobar + beta_now * beta_now)
        cosine = rhobar / rho_now
        sine = beta_now / rho_now
        theta = sine * alpha_now
        rhobar = -cosine * alpha_now
        phi_now = cosine * phibar
        phibar = sine * phibar
        x_vec = x_vec + (phi_now / rho_now)[None, :, None] * w_vec
        w_vec = v_vec - (theta / rho_now)[None, :, None] * w_vec
    all_cols = assign.shape[0]
    natural = lax.axis_index(COL) * tile_cols + jnp.arange(tile_cols, dtype=jnp.int32)
    positions = jnp.arange(all_cols, dtype=jnp.int32)
    where_held = jnp.sum(
        positions[None, :] * (assign[None, :] == natural[:, None]).astype(jnp.int32), axis=1
    )
    share = sources // lax.axis_size("row")
    own_share = lax.dynamic_slice_in_dim(x_vec, lax.axis_index("row") * share, share, 1)
    gathered = collect(own_share, COL, 2)
    gathered = gathered.reshape(2, share, all_cols, tile_size)
    picked = jnp.take(gathered, where_held, axis=2).reshape(2, share, tile_cols * tile_size)
    solution = collect(picked, "row", 1)
    return (solution, phibar)


def solution(mesh):
    split = Mesh(
        mesh.devices.reshape(4, 4, 2, mesh.shape["row"]), ("col_0", "col_1", "col_2", "row")
    )
    placed = (
        P(None, None, "row", COL),
        P("row", COL, None, None, None),
        P("row", COL, None, None, None),
        P("row", COL),
        P(),
    )
    return jax.shard_map(
        on_device, mesh=split, in_specs=placed, out_specs=(P(None, None, COL), P()), check_vma=False
    )
```

profile of v0, /device:TPU:0, one launch (start us, length us, event | category | flops | bytes accessed | tf_op | source)
XLA Modules:
  0.0 301.4 jit_solution(13848021169827376200)
XLA Ops:
  0.6 0.8 convert_element_type.53
  1.4 0.9 broadcast_in_dim.61
  2.3 7.4 %all-to-all-start = ((bf16[32,2,32,128]{3,2,1,0:T(8,128)(2,1)}), bf16[32,2,32,128]{3,2,1,0:T(8,128)(2,1)S(1)}, u32[]{:S(2)}, u32[]{:S(2)}) async-start(bf16[32,2,32,128]{3,2,1,0:T(8,128)(2,1)} %broadcast_in_dim.61), calls=%async_computation | async-start | bytes 1048576 | tf_op jit(solution)/shard_map/all_to_all | solution.py:31
  9.7 0.8 copy.231
  10.6 10.3 %all-to-all-done = bf16[32,2,32,128]{3,2,1,0:T(8,128)(2,1)S(1)} async-done(((bf16[32,2,32,128]{3,2,1,0:T(8,128)(2,1)}), bf16[32,2,32,128]{3,2,1,0:T(8,128)(2,1)S(1)}, u32[]{:S(2)}, u32[]{:S(2)}) %all-to-all-start) | async-done | bytes 524320 | tf_op jit(solution)/shard_map/all_to_all | solution.py:31
  21.5 6.0 %fusion.29 = f32[16,5,2,2,32,128]{5,4,2,1,3,0:T(8,128)S(1)} fusion(bf16[16,5,2,256,128]{4,3,2,1,0:T(8,128)(2,1)} %param.6, bf16[2,32,16,256,1,1]{3,2,1,0,5,4:T(8,128)(2,1)S(1)} %bitcast.189), kind=kOutput, calls=%fused_computation.28 | convolution fusion | flops 671088640 | bytes 16252928 | tf_op jit(solution)/shard_map/ipcnk,dsin->ipcdsk/dot_general | solution.py:69
  28.3 3.3 %fusion.55 = f32[2,2,32,5,256]{4,2,0,1,3:T(8,128)S(1)} fusion(bf16[16,5,2,256,128]{4,3,2,1,0:T(8,128)(2,1)S(1)} %bitcast.181, f32[16,5,1,32,128]{4,3,1,0,2:T(8,128)S(1)} %fusion.48, f32[16,5,1,32,128]{4,3,1,0,2:T(8,128)S(1)} %fusion.50, f32[16,5,128]{2,1,0:T(8,128)S(1)} %fusion.88), kind=kOutput, calls=%fused_computation.59 | convolution fusion | flops 673054720 | bytes 13803520 | tf_op jit(solution)/shard_map/ipcnk,ipdsk->cdspn/dot_general | solution.py:74
  32.0 0.9 broadcast_in_dim.62
  32.9 5.3 %all-to-all-start.1 = ((bf16[4,2,32,1280]{3,2,1,0:T(8,128)(2,1)}), bf16[4,2,32,1280]{3,2,1,0:T(8,128)(2,1)S(1)}, u32[]{:S(2)}, u32[]{:S(2)}) async-start(bf16[4,2,32,1280]{3,2,1,0:T(8,128)(2,1)} %broadcast_in_dim.62), calls=%async_computation.1 | async-start | bytes 1310720 | tf_op jit(solution)/shard_map/all_to_all | solution.py:31
  38.3 8.9 %psum.84 = f32[32]{0:T(128)S(1)} all-reduce(f32[32]{0:T(128)S(1)} %multiply_reduce_fusion.4), channel_id=1, replica_groups=mesh['col_0'=4,'col_1'=4,'col_2'=2,'row'=4] {'col_0'}, use_global_device_ids=true, to_apply=%region_3.0 | all-reduce | flops 32 | bytes 256 | tf_op jit(solution)/shard_map/psum | solution.py:40
  47.2 9.2 %psum.85 = f32[32]{0:T(128)S(1)} all-reduce(f32[32]{0:T(128)S(1)} %psum.84), channel_id=1, replica_groups=mesh['col_0'=4,'col_1'=4,'col_2'=2,'row'=4] {'col_1'}, use_global_device_ids=true, to_apply=%region_4.0 | all-reduce | flops 32 | bytes 256 | tf_op jit(solution)/shard_map/psum | solution.py:40
  56.4 2.4 psum.86
  58.9 10.9 %psum.87 = f32[32]{0:T(128)S(1)} all-reduce(f32[32]{0:T(128)S(1)} %psum.86), channel_id=1, replica_groups=mesh['col_0'=4,'col_1'=4,'col_2'=2,'row'=4] {'row'}, use_global_device_ids=true, to_apply=%region_6.0 | all-reduce | flops 32 | bytes 256 | tf_op jit(solution)/shard_map/psum | solution.py:40
  70.2 10.5 %all_to_all.52 = f32[32,1,32]{2,1,0:T(1,128)S(1)} all-to-all(f32[32,1,32]{2,1,0:T(1,128)S(1)} %broadcast_in_dim.64), channel_id=1, replica_groups=mesh['col_0'=4,'col_1'=4,'col_2'=2,'row'=4] {'col_0','col_1','col_2'}, dimensions={0} | all-to-all | bytes 8192 | tf_op jit(solution)/shard_map/all_to_all | solution.py:31
  80.7 5.3 %fusion.20 = f32[16,5,2,2,32,128]{5,4,1,0,3,2:T(8,128)S(1)} fusion(f32[2,4,5,8,256]{4,3,2,1,0:T(8,128)S(1)} %bitcast.185, f32[32]{0:T(128)S(1)} %sqrt.30, f32[32]{0:T(128)S(1)} %get-tuple-element.29, f32[32]{0:T(128)S(1)} %get-tuple-element.28, bf16[16,5,2,256,128]{4,3,2,1,0:T(8,128)(2,1)} %param.7), kind=kOutput, calls=%fused_computation.25 | convolution fusion | flops 671416320 | bytes 16056704 | tf_op jit(solution)/shard_map/ipcnk,dspn->ipcdsk/dot_general | solution.py:102
  86.0 1.7 fusion.47
  87.7 4.6 %fusion.32 = f32[2,2,32,16,256]{4,2,0,1,3:T(8,128)S(1)} fusion(bf16[16,5,2,256,128]{4,3,2,1,0:T(8,128)(2,1)S(1)} %bitcast.177, f32[16,5,1,32,128]{4,3,1,0,2:T(8,128)} %get-tuple-element.16, f32[16,5,1,32,128]{4,3,1,0,2:T(8,128)S(1)} %get-tuple-element.15, f32[16,5,128]{2,1,0:T(8,128)S(1)} %fusion.88), kind=kOutput, calls=%fused_computation.29 | convolution fusion | flops 673054720 | bytes 15245312 | tf_op jit(solution)/shard_map/ipcnk,ipdsk->cdsin/dot_general | solution.py:113
  93.3 14.5 %all_to_all.53 = bf16[32,2,32,128]{3,2,1,0:T(8,128)(2,1)S(1)} all-to-all(bf16[32,2,32,128]{3,2,1,0:T(8,128)(2,1)S(1)} %copy.245), channel_id=1, replica_groups=mesh['col_0'=4,'col_1'=4,'col_2'=2,'row'=4] {'col_0','col_1','col_2'}, dimensions={0} | all-to-all | bytes 1048576 | tf_op jit(solution)/shard_map/all_to_all | solution.py:19
  108.2 15.0 %all_to_all.54 = bf16[32,2,32,128]{3,2,1,0:T(8,128)(2,1)S(1)} all-to-all(bf16[32,2,32,128]{3,2,1,0:T(8,128)(2,1)S(1)} %broadcast_in_dim.65), channel_id=1, replica_groups=mesh['col_0'=4,'col_1'=4,'col_2'=2,'row'=4] {'col_0','col_1','col_2'}, dimensions={0} | all-to-all | bytes 1048576 | tf_op jit(solution)/shard_map/all_to_all | solution.py:31
  123.8 5.3 %fusion.26 = f32[16,5,2,2,32,128]{5,4,1,0,3,2:T(8,128)S(1)} fusion(bf16[2,32,16,256,1,1]{3,2,1,0,5,4:T(8,128)(2,1)S(1)} %bitcast.187, bf16[16,5,2,256,128]{4,3,2,1,0:T(8,128)(2,1)} %param.6), kind=kOutput, calls=%fused_computation.27 | convolution fusion | flops 671088640 | bytes 16252928 | tf_op jit(solution)/shard_map/ipcnk,dsin->ipcdsk/dot_general | solution.py:69
  130.5 3.3 %fusion.60 = f32[2,2,32,5,256]{4,2,0,1,3:T(8,128)S(1)} fusion(bf16[16,5,2,256,128]{4,3,2,1,0:T(8,128)(2,1)S(1)} %bitcast.183, f32[16,5,1,32,128]{4,3,1,0,2:T(8,128)S(1)} %get-tuple-element.14, f32[16,5,1,32,128]{4,3,1,0,2:T(8,128)S(1)} %get-tuple-element.13, f32[16,5,128]{2,1,0:T(8,128)S(1)} %copy-done.2), kind=kOutput, calls=%fused_computation.60 | convolution fusion | flops 673054720 | bytes 13803520 | tf_op jit(solution)/shard_map/ipcnk,ipdsk->cdspn/dot_general | solution.py:74
  134.1 0.9 broadcast_in_dim.66
  135.0 3.5 %all-to-all-start.5 = ((bf16[4,2,32,1280]{3,2,1,0:T(8,128)(2,1)}), bf16[4,2,32,1280]{3,2,1,0:T(8,128)(2,1)S(1)}, u32[]{:S(2)}, u32[]{:S(2)}) async-start(bf16[4,2,32,1280]{3,2,1,0:T(8,128)(2,1)} %broadcast_in_dim.66), calls=%async_computation.5 | async-start | bytes 1310720 | tf_op jit(solution)/shard_map/all_to_all | solution.py:31
  138.5 8.9 %psum.88 = f32[32]{0:T(128)S(1)} all-reduce(f32[32]{0:T(128)S(1)} %get-tuple-element.9), channel_id=1, replica_groups=mesh['col_0'=4,'col_1'=4,'col_2'=2,'row'=4] {'col_0'}, use_global_device_ids=true, to_apply=%region_11.0 | all-reduce | flops 32 | bytes 256 | tf_op jit(solution)/shard_map/psum | solution.py:40
  147.4 9.2 %psum.89 = f32[32]{0:T(128)S(1)} all-reduce(f32[32]{0:T(128)S(1)} %psum.88), channel_id=1, replica_groups=mesh['col_0'=4,'col_1'=4,'col_2'=2,'row'=4] {'col_1'}, use_global_device_ids=true, to_apply=%region_12.0 | all-reduce | flops 32 | bytes 256 | tf_op jit(solution)/shard_map/psum | solution.py:40
  156.6 2.4 psum.90
  159.1 10.9 %psum.91 = f32[32]{0:T(128)S(1)} all-reduce(f32[32]{0:T(128)S(1)} %psum.90), channel_id=1, replica_groups=mesh['col_0'=4,'col_1'=4,'col_2'=2,'row'=4] {'row'}, use_global_device_ids=true, to_apply=%region_14.0 | all-reduce | flops 32 | bytes 256 | tf_op jit(solution)/shard_map/psum | solution.py:40
  170.1 1.1 multiply_reduce_fusion
  171.2 10.3 %all_to_all.55 = f32[32,1,32]{2,1,0:T(1,128)S(1)} all-to-all(f32[32,1,32]{2,1,0:T(1,128)S(1)} %broadcast_in_dim.67), channel_id=1, replica_groups=mesh['col_0'=4,'col_1'=4,'col_2'=2,'row'=4] {'col_0','col_1','col_2'}, dimensions={0} | all-to-all | bytes 8192 | tf_op jit(solution)/shard_map/all_to_all | solution.py:31
  181.6 5.3 %fusion.23 = f32[16,5,2,2,32,128]{5,4,1,0,3,2:T(8,128)S(1)} fusion(f32[2,4,5,8,256]{4,3,2,1,0:T(8,128)S(1)} %bitcast.188, f32[32]{0:T(128)S(1)} %sqrt.33, f32[32]{0:T(128)S(1)} %sqrt.31, f32[2,4,5,8,256]{4,3,2,1,0:T(8,128)S(1)} %bitcast.186, f32[32]{0:T(128)S(1)} %sqrt.30, f32[32]{0:T(128)S(1)} %get-tuple-element.29, f32[32]{0:T(128)S(1)} %get-tuple-element.28, ...), kind=kOutput, calls=%fused_computation.26 | convolution fusion | flops 671744000 | bytes 16384640 | tf_op jit(solution)/shard_map/ipcnk,dspn->ipcdsk/dot_general | solution.py:102
  188.1 3.5 %fusion.35 = f32[2,2,32,16,256]{4,2,0,1,3:T(8,128)S(1)} fusion(bf16[16,5,2,256,128]{4,3,2,1,0:T(8,128)(2,1)S(1)} %bitcast.179, f32[16,5,1,32,128]{4,3,1,0,2:T(8,128)S(1)} %get-tuple-element.12, f32[16,5,1,32,128]{4,3,1,0,2:T(8,128)S(1)} %get-tuple-element.11, f32[16,5,128]{2,1,0:T(8,128)S(1)} %copy-done.2), kind=kOutput, calls=%fused_computation.30 | convolution fusion | flops 673054720 | bytes 15245312 | tf_op jit(solution)/shard_map/ipcnk,ipdsk->cdsin/dot_general | solution.py:113
  192.3 1.0 copy.262
  193.3 3.9 %all-to-all-start.7 = ((bf16[32,2,32,128]{3,2,1,0:T(8,128)(2,1)}), bf16[32,2,32,128]{3,2,1,0:T(8,128)(2,1)S(1)}, u32[]{:S(2)}, u32[]{:S(2)}) async-start(bf16[32,2,32,128]{3,2,1,0:T(8,128)(2,1)} %copy.262), calls=%async_computation.7 | async-start | bytes 1048576 | tf_op jit(solution)/shard_map/all_to_all | solution.py:19
  197.3 11.1 %all-to-all-done.7 = bf16[32,2,32,128]{3,2,1,0:T(8,128)(2,1)S(1)} async-done(((bf16[32,2,32,128]{3,2,1,0:T(8,128)(2,1)}), bf16[32,2,32,128]{3,2,1,0:T(8,128)(2,1)S(1)}, u32[]{:S(2)}, u32[]{:S(2)}) %all-to-all-start.7) | async-done | bytes 524320 | tf_op jit(solution)/shard_map/all_to_all | solution.py:19
  208.6 8.9 %psum.92 = f32[32]{0:T(128)S(1)} all-reduce(f32[32]{0:T(128)S(1)} %multiply_reduce_fusion.2), channel_id=1, replica_groups=mesh['col_0'=4,'col_1'=4,'col_2'=2,'row'=4] {'col_0'}, use_global_device_ids=true, to_apply=%region_20.0 | all-reduce | flops 32 | bytes 256 | tf_op jit(solution)/shard_map/psum | solution.py:40
  217.6 9.2 %psum.93 = f32[32]{0:T(128)S(1)} all-reduce(f32[32]{0:T(128)S(1)} %psum.92), channel_id=1, replica_groups=mesh['col_0'=4,'col_1'=4,'col_2'=2,'row'=4] {'col_1'}, use_global_device_ids=true, to_apply=%region_21.0 | all-reduce | flops 32 | bytes 256 | tf_op jit(solution)/shard_map/psum | solution.py:40
  226.7 2.4 psum.94
  229.2 7.7 %psum.95 = f32[32]{0:T(128)S(1)} all-reduce(f32[32]{0:T(128)S(1)} %psum.94), channel_id=1, replica_groups=mesh['col_0'=4,'col_1'=4,'col_2'=2,'row'=4] {'row'}, use_global_device_ids=true, to_apply=%region_23.0 | all-reduce | flops 32 | bytes 256 | tf_op jit(solution)/shard_map/psum | solution.py:40
  237.7 1.0 fusion.87
  238.7 1.8 broadcast_in_dim.68
  240.5 4.4 %all-to-all-start.8 = ((f32[32,2,8,1280]{3,2,1,0:T(8,128)}), f32[32,2,8,1280]{3,2,1,0:T(8,128)S(1)}, u32[]{:S(2)}, u32[]{:S(2)}) async-start(f32[32,2,8,1280]{3,2,1,0:T(8,128)} %broadcast_in_dim.68), calls=%async_computation.8 | async-start | bytes 5242880 | tf_op jit(solution)/shard_map/all_to_all | solution.py:31
  245.3 34.1 %all-to-all-done.8 = f32[32,2,8,1280]{3,2,1,0:T(8,128)S(1)} async-done(((f32[32,2,8,1280]{3,2,1,0:T(8,128)}), f32[32,2,8,1280]{3,2,1,0:T(8,128)S(1)}, u32[]{:S(2)}, u32[]{:S(2)}) %all-to-all-start.8) | async-done | bytes 2621472 | tf_op jit(solution)/shard_map/all_to_all | solution.py:31
  279.4 3.0 %copy.263 = f32[2,8,32,1280]{3,2,1,0:T(8,128)} copy(f32[2,8,32,1280]{3,1,0,2:T(8,128)S(1)} %bitcast.184) | data formatting | bytes 5242880 | tf_op jit(solution)/shard_map/transpose | solution.py:24
  282.4 2.7 reshape_reshape.11
  285.1 3.0 %copy.264 = f32[2,8,160,256]{3,1,2,0:T(8,128)} copy(f32[2,8,160,256]{3,2,1,0:T(8,128)S(1)} %reshape_reshape.11) | data formatting | bytes 5242880 | tf_op jit(solution)/shard_map/reshape;reshape | solution.py:144
  288.1 2.3 gather_fusion
  290.5 10.1 %all_to_all.56 = f32[4,2,8,1280]{3,2,1,0:T(8,128)S(1)} all-to-all(f32[4,2,8,1280]{3,2,1,0:T(8,128)S(1)} %broadcast_in_dim.70), channel_id=1, replica_groups=mesh['col_0'=4,'col_1'=4,'col_2'=2,'row'=4] {'row'}, dimensions={0} | all-to-all | bytes 655360 | tf_op jit(solution)/shard_map/all_to_all | solution.py:31
  300.6 0.7 copy.380
  (106 shorter events, 9.4 us)
Async XLA Ops:
  2.3 18.6 %all-to-all-start = ((bf16[32,2,32,128]{3,2,1,0:T(8,128)(2,1)}), bf16[32,2,32,128]{3,2,1,0:T(8,128)(2,1)S(1)}, u32[]{:S(2)}, u32[]{:S(2)}) async-start(bf16[32,2,32,128]{3,2,1,0:T(8,128)(2,1)} %broadcast_in_dim.61), calls=%async_computation | async-start | bytes 1048576 | tf_op jit(solution)/shard_map/all_to_all | solution.py:31
  10.6 77.2 %copy-start.1 = (f32[16,5,128]{2,1,0:T(8,128)}, f32[16,5,128]{2,1,0:T(8,128)S(1)}, u32[]{:S(2)}) copy-start(f32[16,5,128]{2,1,0:T(8,128)S(1)} %fusion.88) | copy-start | bytes 122884
  21.2 6.8 %slice-start.6 = ((s8[10485760]{0:T(1024)(128)(4,1)}), s8[2097152]{0:T(1024)(128)(4,1)S(1)}, s32[]{:S(2)}) async-start(s8[10485760]{0:T(1024)(128)(4,1)} %bitcast.180), calls=%async_computation.16 | async-start | bytes 4194304
  21.4 6.6 %slice-start.7 = ((s8[10485760]{0:T(1024)(128)(4,1)}), s8[4194304]{0:T(1024)(128)(4,1)S(1)}, s32[]{:S(2)}) async-start(s8[10485760]{0:T(1024)(128)(4,1)} %bitcast.180), calls=%async_computation.17 | async-start | bytes 8388608
  21.5 6.9 %slice-start.8 = ((s8[10485760]{0:T(1024)(128)(4,1)}), s8[4194304]{0:T(1024)(128)(4,1)S(1)}, s32[]{:S(2)}) async-start(s8[10485760]{0:T(1024)(128)(4,1)} %bitcast.180), calls=%async_computation.18 | async-start | bytes 8388608
  31.6 6.6 %copy-start = (f32[2,32,1,128]{3,2,1,0:T(1,128)S(1)}, f32[2,32,1,128]{3,2,1,0:T(1,128)}, u32[]{:S(2)}) copy-start(f32[2,32,1,128]{3,2,1,0:T(1,128)} %param.5) | copy-start | bytes 98308
  32.9 36.9 %all-to-all-start.1 = ((bf16[4,2,32,1280]{3,2,1,0:T(8,128)(2,1)}), bf16[4,2,32,1280]{3,2,1,0:T(8,128)(2,1)S(1)}, u32[]{:S(2)}, u32[]{:S(2)}) async-start(bf16[4,2,32,1280]{3,2,1,0:T(8,128)(2,1)} %broadcast_in_dim.62), calls=%async_computation.1 | async-start | bytes 1310720 | tf_op jit(solution)/shard_map/all_to_all | solution.py:31
  69.8 17.9 %slice-start = ((s8[10485760]{0:T(1024)(128)(4,1)}), s8[2097152]{0:T(1024)(128)(4,1)S(1)}, s32[]{:S(2)}) async-start(s8[10485760]{0:T(1024)(128)(4,1)} %bitcast.176), calls=%async_computation.10 | async-start | bytes 4194304
  80.7 7.1 %slice-start.1 = ((s8[10485760]{0:T(1024)(128)(4,1)}), s8[4194304]{0:T(1024)(128)(4,1)S(1)}, s32[]{:S(2)}) async-start(s8[10485760]{0:T(1024)(128)(4,1)} %bitcast.176), calls=%async_computation.11 | async-start | bytes 8388608
  80.7 7.1 %slice-start.2 = ((s8[10485760]{0:T(1024)(128)(4,1)}), s8[4194304]{0:T(1024)(128)(4,1)S(1)}, s32[]{:S(2)}) async-start(s8[10485760]{0:T(1024)(128)(4,1)} %bitcast.176), calls=%async_computation.12 | async-start | bytes 8388608
  123.2 6.5 %slice-start.9 = ((s8[10485760]{0:T(1024)(128)(4,1)}), s8[2097152]{0:T(1024)(128)(4,1)S(1)}, s32[]{:S(2)}) async-start(s8[10485760]{0:T(1024)(128)(4,1)} %bitcast.182), calls=%async_computation.19 | async-start | bytes 4194304
  123.8 6.0 %slice-start.10 = ((s8[10485760]{0:T(1024)(128)(4,1)}), s8[4194304]{0:T(1024)(128)(4,1)S(1)}, s32[]{:S(2)}) async-start(s8[10485760]{0:T(1024)(128)(4,1)} %bitcast.182), calls=%async_computation.20 | async-start | bytes 8388608
  123.8 6.7 %slice-start.11 = ((s8[10485760]{0:T(1024)(128)(4,1)}), s8[4194304]{0:T(1024)(128)(4,1)S(1)}, s32[]{:S(2)}) async-start(s8[10485760]{0:T(1024)(128)(4,1)} %bitcast.182), calls=%async_computation.21 | async-start | bytes 8388608
  129.1 1.4 copy-start.2
  135.0 34.9 %all-to-all-start.5 = ((bf16[4,2,32,1280]{3,2,1,0:T(8,128)(2,1)}), bf16[4,2,32,1280]{3,2,1,0:T(8,128)(2,1)S(1)}, u32[]{:S(2)}, u32[]{:S(2)}) async-start(bf16[4,2,32,1280]{3,2,1,0:T(8,128)(2,1)} %broadcast_in_dim.66), calls=%async_computation.5 | async-start | bytes 1310720 | tf_op jit(solution)/shard_map/all_to_all | solution.py:31
  170.0 17.6 %slice-start.3 = ((s8[10485760]{0:T(1024)(128)(4,1)}), s8[2097152]{0:T(1024)(128)(4,1)S(1)}, s32[]{:S(2)}) async-start(s8[10485760]{0:T(1024)(128)(4,1)} %bitcast.178), calls=%async_computation.13 | async-start | bytes 4194304
  181.5 6.0 %slice-start.4 = ((s8[10485760]{0:T(1024)(128)(4,1)}), s8[4194304]{0:T(1024)(128)(4,1)S(1)}, s32[]{:S(2)}) async-start(s8[10485760]{0:T(1024)(128)(4,1)} %bitcast.178), calls=%async_computation.14 | async-start | bytes 8388608
  181.6 6.5 %slice-start.5 = ((s8[10485760]{0:T(1024)(128)(4,1)}), s8[4194304]{0:T(1024)(128)(4,1)S(1)}, s32[]{:S(2)}) async-start(s8[10485760]{0:T(1024)(128)(4,1)} %bitcast.178), calls=%async_computation.15 | async-start | bytes 8388608
  193.3 15.1 %all-to-all-start.7 = ((bf16[32,2,32,128]{3,2,1,0:T(8,128)(2,1)}), bf16[32,2,32,128]{3,2,1,0:T(8,128)(2,1)S(1)}, u32[]{:S(2)}, u32[]{:S(2)}) async-start(bf16[32,2,32,128]{3,2,1,0:T(8,128)(2,1)} %copy.262), calls=%async_computation.7 | async-start | bytes 1048576 | tf_op jit(solution)/shard_map/all_to_all | solution.py:19
  240.5 4.4 %copy-start.3 = (s32[160]{0:T(256)S(1)}, s32[160]{0:T(256)}, u32[]{:S(2)}) copy-start(s32[160]{0:T(256)} %param.9) | copy-start | bytes 1924
  240.5 38.8 %all-to-all-start.8 = ((f32[32,2,8,1280]{3,2,1,0:T(8,128)}), f32[32,2,8,1280]{3,2,1,0:T(8,128)S(1)}, u32[]{:S(2)}, u32[]{:S(2)}) async-start(f32[32,2,8,1280]{3,2,1,0:T(8,128)} %broadcast_in_dim.68), calls=%async_computation.8 | async-start | bytes 5242880 | tf_op jit(solution)/shard_map/all_to_all | solution.py:31
where the time goes:
time: 303 us; the launch traced here: 301 us
  blocking collectives  152 us (50%)
  waiting for transfers between devices  55.5 us (18%)
  matrix products  36.5 us (12%)
  starting transfers between devices  24.5 us (8%)
  local copies, waits for them, and re-layouts  23 us (8%)
  other arithmetic  8.98 us (3%)
    psum x12, blocking collectives, by_axis(): x = lax.psum(x, axis)  91.2 us
    all_to_all x4, blocking collectives, copy_for_each(): return lax.all_to_all(copies, axis, split_axis=0, concat_axis=0, tiled=True)  46 us
    all_to_all x4, waiting for transfers between devices, copy_for_each(): return lax.all_to_all(copies, axis, split_axis=0, concat_axis=0, tiled=True)  44.4 us
    all_to_all x4, starting transfers between devices, copy_for_each(): return lax.all_to_all(copies, axis, split_axis=0, concat_axis=0, tiled=True)  20.6 us
    all_to_all x1, blocking collectives, sent_and_summed(): tiles = lax.all_to_all(cut_along(x, dim, devices), axis, 0, 0, tiled=True)  14.5 us
    dot_general x2, matrix products, adjoint_terms(): jnp.einsum('ipcnk,dsin->ipcdsk', u_factor, data_b, preferred_element_type...  11.3 us
    all_to_all x1, waiting for transfers between devices, sent_and_summed(): tiles = lax.all_to_all(cut_along(x, dim, devices), axis, 0, 0, tiled=True)  11.1 us
    dot_general x2, matrix products, on_device(): jnp.einsum('ipcnk,dspn->ipcdsk', v_factor, model_b, preferred_element_typ...  10.6 us
  transfers between devices with their start and end apart: 5, of which 3 were waited for; matrix products, arithmetic and copies ran while one was open for 0% of the time, Pallas kernels for 0%

commit v1 on v0

--- a/solution.py
+++ b/solution.py
@@ -37,7 +37,8 @@
 
 def by_axis(x, axes):
     for axis in axes:
-        x = lax.psum(x, axis)
+        shards = lax.all_gather(x, axis)
+        x = jnp.sum(shards, axis=0)
     return x
 
 

time: 303 us -> 312 us (1.030)
  local copies, waits for them, and re-layouts: 23 us -> 29.4 us
    psum x12 -> x0, blocking collectives: 91.2 us -> none  [by_axis(): x = lax.psum(x, axis)]
    unnamed x0 -> x12, blocking collectives: none -> 91 us
    unnamed x33 -> x69, local copies, waits for them, and re-layouts: 2.33 us -> 7.7 us
  transfers between devices with their start and end apart: 5 -> 5, of which waited for: 3 -> 3; matrix products, arithmetic and copies ran while one was open for 0% -> 2% of each run, Pallas kernels for 0% -> 0%
where the time goes in v1:
time: 312 us; the launch traced here: 311 us
  blocking collectives  151 us (48%)
  waiting for transfers between devices  55.7 us (18%)
  matrix products  36.5 us (12%)
  local copies, waits for them, and re-layouts  29.4 us (9%)
  starting transfers between devices  24.3 us (8%)
  other arithmetic  9.24 us (3%)
  between operations  4 us (1%)
    unnamed x12, blocking collectives  91 us
    all_to_all x4, blocking collectives, copy_for_each(): return lax.all_to_all(copies, axis, split_axis=0, concat_axis=0, tiled=True)  46 us
    all_to_all x4, waiting for transfers between devices, copy_for_each(): return lax.all_to_all(copies, axis, split_axis=0, concat_axis=0, tiled=True)  44.6 us
    all_to_all x4, starting transfers between devices, copy_for_each(): return lax.all_to_all(copies, axis, split_axis=0, concat_axis=0, tiled=True)  20.4 us
    all_to_all x1, blocking collectives, sent_and_summed(): tiles = lax.all_to_all(cut_along(x, dim, devices), axis, 0, 0, tiled=True)  14.5 us
    dot_general x2, matrix products, adjoint_terms(): jnp.einsum('ipcnk,dsin->ipcdsk', u_factor, data_b, preferred_element_type...  11.3 us
    all_to_all x1, waiting for transfers between devices, sent_and_summed(): tiles = lax.all_to_all(cut_along(x, dim, devices), axis, 0, 0, tiled=True)  11.1 us
    dot_general x2, matrix products, on_device(): jnp.einsum('ipcnk,dspn->ipcdsk', v_factor, model_b, preferred_element_typ...  10.6 us
  transfers between devices with their start and end apart: 5, of which 3 were waited for; matrix products, arithmetic and copies ran while one was open for 2% of the time, Pallas kernels for 0%

profile of v1, /device:TPU:0, one launch (start us, length us, event | category | flops | bytes accessed | tf_op | source)
XLA Modules:
  0.0 310.5 jit_solution(839607295782500050)
XLA Ops:
  0.6 0.8 convert_element_type.53
  1.4 0.9 broadcast_in_dim.61
  2.3 7.4 %all-to-all-start = ((bf16[32,2,32,128]{3,2,1,0:T(8,128)(2,1)}), bf16[32,2,32,128]{3,2,1,0:T(8,128)(2,1)S(1)}, u32[]{:S(2)}, u32[]{:S(2)}) async-start(bf16[32,2,32,128]{3,2,1,0:T(8,128)(2,1)} %broadcast_in_dim.61), calls=%async_computation | async-start | bytes 1048576 | tf_op jit(solution)/shard_map/all_to_all | solution.py:31
  9.7 0.8 copy.231
  10.6 10.3 %all-to-all-done = bf16[32,2,32,128]{3,2,1,0:T(8,128)(2,1)S(1)} async-done(((bf16[32,2,32,128]{3,2,1,0:T(8,128)(2,1)}), bf16[32,2,32,128]{3,2,1,0:T(8,128)(2,1)S(1)}, u32[]{:S(2)}, u32[]{:S(2)}) %all-to-all-start) | async-done | bytes 524320 | tf_op jit(solution)/shard_map/all_to_all | solution.py:31
  21.5 6.0 %fusion.29 = f32[16,5,2,2,32,128]{5,4,2,1,3,0:T(8,128)S(1)} fusion(bf16[16,5,2,256,128]{4,3,2,1,0:T(8,128)(2,1)} %param.6, bf16[2,32,16,256,1,1]{3,2,1,0,5,4:T(8,128)(2,1)S(1)} %bitcast.193), kind=kOutput, calls=%fused_computation.28 | convolution fusion | flops 671088640 | bytes 16252928 | tf_op jit(solution)/shard_map/ipcnk,dsin->ipcdsk/dot_general | solution.py:70
  28.3 3.3 %fusion.55 = f32[2,2,32,5,256]{4,2,0,1,3:T(8,128)S(1)} fusion(bf16[16,5,2,256,128]{4,3,2,1,0:T(8,128)(2,1)S(1)} %bitcast.185, f32[16,5,1,32,128]{4,3,1,0,2:T(8,128)S(1)} %fusion.48, f32[16,5,1,32,128]{4,3,1,0,2:T(8,128)S(1)} %fusion.50, f32[16,5,128]{2,1,0:T(8,128)S(1)} %fusion.88), kind=kOutput, calls=%fused_computation.59 | convolution fusion | flops 673054720 | bytes 13803520 | tf_op jit(solution)/shard_map/ipcnk,ipdsk->cdspn/dot_general | solution.py:75
  32.1 0.9 broadcast_in_dim.62
  32.9 5.3 %all-to-all-start.1 = ((bf16[4,2,32,1280]{3,2,1,0:T(8,128)(2,1)}), bf16[4,2,32,1280]{3,2,1,0:T(8,128)(2,1)S(1)}, u32[]{:S(2)}, u32[]{:S(2)}) async-start(bf16[4,2,32,1280]{3,2,1,0:T(8,128)(2,1)} %broadcast_in_dim.62), calls=%async_computation.1 | async-start | bytes 1310720 | tf_op jit(solution)/shard_map/all_to_all | solution.py:31
  39.9 8.8 %all-reduce = f32[128]{0:T(128)S(1)} all-reduce(f32[128]{0:T(128)S(1)} %dynamic-update-slice), channel_id=2, replica_groups=mesh['col_0'=4,'col_1'=4,'col_2'=2,'row'=4] {'col_0'}, use_global_device_ids=true, to_apply=%add | all-reduce | flops 128 | bytes 1024
  50.3 9.2 %all-reduce.1 = f32[128]{0:T(128)S(1)} all-reduce(f32[128]{0:T(128)S(1)} %dynamic-update-slice.1), channel_id=3, replica_groups=mesh['col_0'=4,'col_1'=4,'col_2'=2,'row'=4] {'col_1'}, use_global_device_ids=true, to_apply=%add.1 | all-reduce | flops 128 | bytes 1024
  61.1 2.4 all-reduce.2
  65.3 10.9 %all-reduce.3 = f32[128]{0:T(128)S(1)} all-reduce(f32[128]{0:T(128)S(1)} %dynamic-update-slice.3), channel_id=5, replica_groups=mesh['col_0'=4,'col_1'=4,'col_2'=2,'row'=4] {'row'}, use_global_device_ids=true, to_apply=%add.3 | all-reduce | flops 128 | bytes 1024
  76.7 10.5 %all_to_all.55 = f32[32,1,32]{2,1,0:T(1,128)S(1)} all-to-all(f32[32,1,32]{2,1,0:T(1,128)S(1)} %broadcast_in_dim.64), channel_id=1, replica_groups=mesh['col_0'=4,'col_1'=4,'col_2'=2,'row'=4] {'col_0','col_1','col_2'}, dimensions={0} | all-to-all | bytes 8192 | tf_op jit(solution)/shard_map/all_to_all | solution.py:31
  87.2 5.3 %fusion.20 = f32[16,5,2,2,32,128]{5,4,1,0,3,2:T(8,128)S(1)} fusion(f32[2,4,5,8,256]{4,3,2,1,0:T(8,128)S(1)} %bitcast.189, f32[32]{0:T(128)S(1)} %sqrt.88, f32[32]{0:T(128)S(1)} %get-tuple-element.29, f32[32]{0:T(128)S(1)} %get-tuple-element.28, bf16[16,5,2,256,128]{4,3,2,1,0:T(8,128)(2,1)} %param.7), kind=kOutput, calls=%fused_computation.25 | convolution fusion | flops 671416320 | bytes 16056704 | tf_op jit(solution)/shard_map/ipcnk,dspn->ipcdsk/dot_general | solution.py:103
  92.5 1.7 fusion.47
  94.2 4.6 %fusion.32 = f32[2,2,32,16,256]{4,2,0,1,3:T(8,128)S(1)} fusion(bf16[16,5,2,256,128]{4,3,2,1,0:T(8,128)(2,1)S(1)} %bitcast.181, f32[16,5,1,32,128]{4,3,1,0,2:T(8,128)} %get-tuple-element.16, f32[16,5,1,32,128]{4,3,1,0,2:T(8,128)S(1)} %get-tuple-element.15, f32[16,5,128]{2,1,0:T(8,128)S(1)} %fusion.88), kind=kOutput, calls=%fused_computation.29 | convolution fusion | flops 673054720 | bytes 15245312 | tf_op jit(solution)/shard_map/ipcnk,ipdsk->cdsin/dot_general | solution.py:114
  99.8 14.5 %all_to_all.52 = bf16[32,2,32,128]{3,2,1,0:T(8,128)(2,1)S(1)} all-to-all(bf16[32,2,32,128]{3,2,1,0:T(8,128)(2,1)S(1)} %copy.245), channel_id=1, replica_groups=mesh['col_0'=4,'col_1'=4,'col_2'=2,'row'=4] {'col_0','col_1','col_2'}, dimensions={0} | all-to-all | bytes 1048576 | tf_op jit(solution)/shard_map/all_to_all | solution.py:19
  114.7 15.0 %all_to_all.53 = bf16[32,2,32,128]{3,2,1,0:T(8,128)(2,1)S(1)} all-to-all(bf16[32,2,32,128]{3,2,1,0:T(8,128)(2,1)S(1)} %broadcast_in_dim.65), channel_id=1, replica_groups=mesh['col_0'=4,'col_1'=4,'col_2'=2,'row'=4] {'col_0','col_1','col_2'}, dimensions={0} | all-to-all | bytes 1048576 | tf_op jit(solution)/shard_map/all_to_all | solution.py:31
  130.3 5.3 %fusion.26 = f32[16,5,2,2,32,128]{5,4,1,0,3,2:T(8,128)S(1)} fusion(bf16[2,32,16,256,1,1]{3,2,1,0,5,4:T(8,128)(2,1)S(1)} %bitcast.191, bf16[16,5,2,256,128]{4,3,2,1,0:T(8,128)(2,1)} %param.6), kind=kOutput, calls=%fused_computation.27 | convolution fusion | flops 671088640 | bytes 16252928 | tf_op jit(solution)/shard_map/ipcnk,dsin->ipcdsk/dot_general | solution.py:70
  136.9 3.3 %fusion.60 = f32[2,2,32,5,256]{4,2,0,1,3:T(8,128)S(1)} fusion(bf16[16,5,2,256,128]{4,3,2,1,0:T(8,128)(2,1)S(1)} %bitcast.187, f32[16,5,1,32,128]{4,3,1,0,2:T(8,128)S(1)} %get-tuple-element.14, f32[16,5,1,32,128]{4,3,1,0,2:T(8,128)S(1)} %get-tuple-element.13, f32[16,5,128]{2,1,0:T(8,128)S(1)} %copy-done.2), kind=kOutput, calls=%fused_computation.60 | convolution fusion | flops 673054720 | bytes 13803520 | tf_op jit(solution)/shard_map/ipcnk,ipdsk->cdspn/dot_general | solution.py:75
  140.6 0.9 broadcast_in_dim.66
  141.5 3.5 %all-to-all-start.5 = ((bf16[4,2,32,1280]{3,2,1,0:T(8,128)(2,1)}), bf16[4,2,32,1280]{3,2,1,0:T(8,128)(2,1)S(1)}, u32[]{:S(2)}, u32[]{:S(2)}) async-start(bf16[4,2,32,1280]{3,2,1,0:T(8,128)(2,1)} %broadcast_in_dim.66), calls=%async_computation.5 | async-start | bytes 1310720 | tf_op jit(solution)/shard_map/all_to_all | solution.py:31
  145.2 8.8 %all-reduce.4 = f32[128]{0:T(128)S(1)} all-reduce(f32[128]{0:T(128)S(1)} %dynamic-update-slice.4), channel_id=6, replica_groups=mesh['col_0'=4,'col_1'=4,'col_2'=2,'row'=4] {'col_0'}, use_global_device_ids=true, to_apply=%add.4 | all-reduce | flops 128 | bytes 1024
  154.4 9.2 %all-reduce.5 = f32[128]{0:T(128)S(1)} all-reduce(f32[128]{0:T(128)S(1)} %dynamic-update-slice.5), channel_id=7, replica_groups=mesh['col_0'=4,'col_1'=4,'col_2'=2,'row'=4] {'col_1'}, use_global_device_ids=true, to_apply=%add.5 | all-reduce | flops 128 | bytes 1024
  164.0 2.4 all-reduce.6
  166.8 10.8 %all-reduce.7 = f32[128]{0:T(128)S(1)} all-reduce(f32[128]{0:T(128)S(1)} %dynamic-update-slice.7), channel_id=9, replica_groups=mesh['col_0'=4,'col_1'=4,'col_2'=2,'row'=4] {'row'}, use_global_device_ids=true, to_apply=%add.7 | all-reduce | flops 128 | bytes 1024
  177.9 1.1 multiply_reduce_fusion
  179.0 10.3 %all_to_all.56 = f32[32,1,32]{2,1,0:T(1,128)S(1)} all-to-all(f32[32,1,32]{2,1,0:T(1,128)S(1)} %broadcast_in_dim.67), channel_id=1, replica_groups=mesh['col_0'=4,'col_1'=4,'col_2'=2,'row'=4] {'col_0','col_1','col_2'}, dimensions={0} | all-to-all | bytes 8192 | tf_op jit(solution)/shard_map/all_to_all | solution.py:31
  189.4 5.3 %fusion.23 = f32[16,5,2,2,32,128]{5,4,1,0,3,2:T(8,128)S(1)} fusion(f32[2,4,5,8,256]{4,3,2,1,0:T(8,128)S(1)} %bitcast.192, f32[32]{0:T(128)S(1)} %sqrt.91, f32[32]{0:T(128)S(1)} %sqrt.89, f32[2,4,5,8,256]{4,3,2,1,0:T(8,128)S(1)} %bitcast.190, f32[32]{0:T(128)S(1)} %sqrt.88, f32[32]{0:T(128)S(1)} %get-tuple-element.29, f32[32]{0:T(128)S(1)} %get-tuple-element.28, ...), kind=kOutput, calls=%fused_computation.26 | convolution fusion | flops 671744000 | bytes 16384640 | tf_op jit(solution)/shard_map/ipcnk,dspn->ipcdsk/dot_general | solution.py:103
  195.9 3.5 %fusion.35 = f32[2,2,32,16,256]{4,2,0,1,3:T(8,128)S(1)} fusion(bf16[16,5,2,256,128]{4,3,2,1,0:T(8,128)(2,1)S(1)} %bitcast.183, f32[16,5,1,32,128]{4,3,1,0,2:T(8,128)S(1)} %get-tuple-element.12, f32[16,5,1,32,128]{4,3,1,0,2:T(8,128)S(1)} %get-tuple-element.11, f32[16,5,128]{2,1,0:T(8,128)S(1)} %copy-done.2), kind=kOutput, calls=%fused_computation.30 | convolution fusion | flops 673054720 | bytes 15245312 | tf_op jit(solution)/shard_map/ipcnk,ipdsk->cdsin/dot_general | solution.py:114
  200.1 1.0 copy.262
  201.1 3.9 %all-to-all-start.7 = ((bf16[32,2,32,128]{3,2,1,0:T(8,128)(2,1)}), bf16[32,2,32,128]{3,2,1,0:T(8,128)(2,1)S(1)}, u32[]{:S(2)}, u32[]{:S(2)}) async-start(bf16[32,2,32,128]{3,2,1,0:T(8,128)(2,1)} %copy.262), calls=%async_computation.7 | async-start | bytes 1048576 | tf_op jit(solution)/shard_map/all_to_all | solution.py:19
  205.1 11.1 %all-to-all-done.7 = bf16[32,2,32,128]{3,2,1,0:T(8,128)(2,1)S(1)} async-done(((bf16[32,2,32,128]{3,2,1,0:T(8,128)(2,1)}), bf16[32,2,32,128]{3,2,1,0:T(8,128)(2,1)S(1)}, u32[]{:S(2)}, u32[]{:S(2)}) %all-to-all-start.7) | async-done | bytes 524320 | tf_op jit(solution)/shard_map/all_to_all | solution.py:19
  216.7 8.9 %all-reduce.8 = f32[128]{0:T(128)S(1)} all-reduce(f32[128]{0:T(128)S(1)} %dynamic-update-slice.8), channel_id=10, replica_groups=mesh['col_0'=4,'col_1'=4,'col_2'=2,'row'=4] {'col_0'}, use_global_device_ids=true, to_apply=%add.8 | all-reduce | flops 128 | bytes 1024
  226.0 9.2 %all-reduce.9 = f32[128]{0:T(128)S(1)} all-reduce(f32[128]{0:T(128)S(1)} %dynamic-update-slice.9), channel_id=11, replica_groups=mesh['col_0'=4,'col_1'=4,'col_2'=2,'row'=4] {'col_1'}, use_global_device_ids=true, to_apply=%add.9 | all-reduce | flops 128 | bytes 1024
  235.5 2.4 all-reduce.10
  238.3 7.7 %all-reduce.11 = f32[128]{0:T(128)S(1)} all-reduce(f32[128]{0:T(128)S(1)} %dynamic-update-slice.11), channel_id=13, replica_groups=mesh['col_0'=4,'col_1'=4,'col_2'=2,'row'=4] {'row'}, use_global_device_ids=true, to_apply=%add.11 | all-reduce | flops 128 | bytes 1024
  246.9 1.0 fusion.87
  247.9 1.8 broadcast_in_dim.68
  249.7 4.2 %all-to-all-start.8 = ((f32[32,2,8,1280]{3,2,1,0:T(8,128)}), f32[32,2,8,1280]{3,2,1,0:T(8,128)S(1)}, u32[]{:S(2)}, u32[]{:S(2)}) async-start(f32[32,2,8,1280]{3,2,1,0:T(8,128)} %broadcast_in_dim.68), calls=%async_computation.8 | async-start | bytes 5242880 | tf_op jit(solution)/shard_map/all_to_all | solution.py:31
  254.2 34.3 %all-to-all-done.8 = f32[32,2,8,1280]{3,2,1,0:T(8,128)S(1)} async-done(((f32[32,2,8,1280]{3,2,1,0:T(8,128)}), f32[32,2,8,1280]{3,2,1,0:T(8,128)S(1)}, u32[]{:S(2)}, u32[]{:S(2)}) %all-to-all-start.8) | async-done | bytes 2621472 | tf_op jit(solution)/shard_map/all_to_all | solution.py:31
  288.5 3.0 copy.263
  291.6 2.7 reshape_reshape.11
  294.3 3.0 copy.264
  297.3 2.3 gather_fusion
  299.7 10.1 %all_to_all.54 = f32[4,2,8,1280]{3,2,1,0:T(8,128)S(1)} all-to-all(f32[4,2,8,1280]{3,2,1,0:T(8,128)S(1)} %broadcast_in_dim.70), channel_id=1, replica_groups=mesh['col_0'=4,'col_1'=4,'col_2'=2,'row'=4] {'row'}, dimensions={0} | all-to-all | bytes 655360 | tf_op jit(solution)/shard_map/all_to_all | solution.py:31
  309.8 0.7 copy.380
  (166 shorter events, 16.0 us)
Async XLA Ops:
  2.3 18.6 %all-to-all-start = ((bf16[32,2,32,128]{3,2,1,0:T(8,128)(2,1)}), bf16[32,2,32,128]{3,2,1,0:T(8,128)(2,1)S(1)}, u32[]{:S(2)}, u32[]{:S(2)}) async-start(bf16[32,2,32,128]{3,2,1,0:T(8,128)(2,1)} %broadcast_in_dim.61), calls=%async_computation | async-start | bytes 1048576 | tf_op jit(solution)/shard_map/all_to_all | solution.py:31
  10.6 83.6 %copy-start.1 = (f32[16,5,128]{2,1,0:T(8,128)}, f32[16,5,128]{2,1,0:T(8,128)S(1)}, u32[]{:S(2)}) copy-start(f32[16,5,128]{2,1,0:T(8,128)S(1)} %fusion.88) | copy-start | bytes 122884
  21.2 6.8 %slice-start.6 = ((s8[10485760]{0:T(1024)(128)(4,1)}), s8[2097152]{0:T(1024)(128)(4,1)S(1)}, s32[]{:S(2)}) async-start(s8[10485760]{0:T(1024)(128)(4,1)} %bitcast.184), calls=%async_computation.16 | async-start | bytes 4194304
  21.4 6.6 %slice-start.7 = ((s8[10485760]{0:T(1024)(128)(4,1)}), s8[4194304]{0:T(1024)(128)(4,1)S(1)}, s32[]{:S(2)}) async-start(s8[10485760]{0:T(1024)(128)(4,1)} %bitcast.184), calls=%async_computation.17 | async-start | bytes 8388608
  21.5 6.9 %slice-start.8 = ((s8[10485760]{0:T(1024)(128)(4,1)}), s8[4194304]{0:T(1024)(128)(4,1)S(1)}, s32[]{:S(2)}) async-start(s8[10485760]{0:T(1024)(128)(4,1)} %bitcast.184), calls=%async_computation.18 | async-start | bytes 8388608
  31.6 6.7 %copy-start.7 = (u32[128]{0:T(128)S(1)}, u32[128]{0:T(128)}, u32[]{:S(2)}) copy-start(u32[128]{0:T(128)} %constant.51) | copy-start | bytes 1540
  31.6 7.9 %copy-start = (f32[2,32,1,128]{3,2,1,0:T(1,128)S(1)}, f32[2,32,1,128]{3,2,1,0:T(1,128)}, u32[]{:S(2)}) copy-start(f32[2,32,1,128]{3,2,1,0:T(1,128)} %param.5) | copy-start | bytes 98308
  31.6 17.2 %copy-start.6 = (u32[128]{0:T(128)S(1)}, u32[128]{0:T(128)}, u32[]{:S(2)}) copy-start(u32[128]{0:T(128)} %constant.56) | copy-start | bytes 1540
  31.6 28.0 %copy-start.5 = (u32[128]{0:T(128)S(1)}, u32[128]{0:T(128)}, u32[]{:S(2)}) copy-start(u32[128]{0:T(128)} %constant.61) | copy-start | bytes 1540
  31.6 32.0 %copy-start.4 = (u32[128]{0:T(128)S(1)}, u32[128]{0:T(128)}, u32[]{:S(2)}) copy-start(u32[128]{0:T(128)} %constant.66) | copy-start | bytes 1540
  32.9 43.4 %all-to-all-start.1 = ((bf16[4,2,32,1280]{3,2,1,0:T(8,128)(2,1)}), bf16[4,2,32,1280]{3,2,1,0:T(8,128)(2,1)S(1)}, u32[]{:S(2)}, u32[]{:S(2)}) async-start(bf16[4,2,32,1280]{3,2,1,0:T(8,128)(2,1)} %broadcast_in_dim.62), calls=%async_computation.1 | async-start | bytes 1310720 | tf_op jit(solution)/shard_map/all_to_all | solution.py:31
  76.3 17.9 %slice-start = ((s8[10485760]{0:T(1024)(128)(4,1)}), s8[2097152]{0:T(1024)(128)(4,1)S(1)}, s32[]{:S(2)}) async-start(s8[10485760]{0:T(1024)(128)(4,1)} %bitcast.180), calls=%async_computation.10 | async-start | bytes 4194304
  87.2 7.1 %slice-start.1 = ((s8[10485760]{0:T(1024)(128)(4,1)}), s8[4194304]{0:T(1024)(128)(4,1)S(1)}, s32[]{:S(2)}) async-start(s8[10485760]{0:T(1024)(128)(4,1)} %bitcast.180), calls=%async_computation.11 | async-start | bytes 8388608
  87.2 7.1 %slice-start.2 = ((s8[10485760]{0:T(1024)(128)(4,1)}), s8[4194304]{0:T(1024)(128)(4,1)S(1)}, s32[]{:S(2)}) async-start(s8[10485760]{0:T(1024)(128)(4,1)} %bitcast.180), calls=%async_computation.12 | async-start | bytes 8388608
  129.7 6.5 %slice-start.9 = ((s8[10485760]{0:T(1024)(128)(4,1)}), s8[2097152]{0:T(1024)(128)(4,1)S(1)}, s32[]{:S(2)}) async-start(s8[10485760]{0:T(1024)(128)(4,1)} %bitcast.186), calls=%async_computation.19 | async-start | bytes 4194304
  130.3 6.0 %slice-start.10 = ((s8[10485760]{0:T(1024)(128)(4,1)}), s8[4194304]{0:T(1024)(128)(4,1)S(1)}, s32[]{:S(2)}) async-start(s8[10485760]{0:T(1024)(128)(4,1)} %bitcast.186), calls=%async_computation.20 | async-start | bytes 8388608
  130.3 6.7 %slice-start.11 = ((s8[10485760]{0:T(1024)(128)(4,1)}), s8[4194304]{0:T(1024)(128)(4,1)S(1)}, s32[]{:S(2)}) async-start(s8[10485760]{0:T(1024)(128)(4,1)} %bitcast.186), calls=%async_computation.21 | async-start | bytes 8388608
  135.6 1.4 copy-start.2
  141.5 36.3 %all-to-all-start.5 = ((bf16[4,2,32,1280]{3,2,1,0:T(8,128)(2,1)}), bf16[4,2,32,1280]{3,2,1,0:T(8,128)(2,1)S(1)}, u32[]{:S(2)}, u32[]{:S(2)}) async-start(bf16[4,2,32,1280]{3,2,1,0:T(8,128)(2,1)} %broadcast_in_dim.66), calls=%async_computation.5 | async-start | bytes 1310720 | tf_op jit(solution)/shard_map/all_to_all | solution.py:31
  177.8 17.6 %slice-start.3 = ((s8[10485760]{0:T(1024)(128)(4,1)}), s8[2097152]{0:T(1024)(128)(4,1)S(1)}, s32[]{:S(2)}) async-start(s8[10485760]{0:T(1024)(128)(4,1)} %bitcast.182), calls=%async_computation.13 | async-start | bytes 4194304
  189.4 6.0 %slice-start.4 = ((s8[10485760]{0:T(1024)(128)(4,1)}), s8[4194304]{0:T(1024)(128)(4,1)S(1)}, s32[]{:S(2)}) async-start(s8[10485760]{0:T(1024)(128)(4,1)} %bitcast.182), calls=%async_computation.14 | async-start | bytes 8388608
  189.4 6.5 %slice-start.5 = ((s8[10485760]{0:T(1024)(128)(4,1)}), s8[4194304]{0:T(1024)(128)(4,1)S(1)}, s32[]{:S(2)}) async-start(s8[10485760]{0:T(1024)(128)(4,1)} %bitcast.182), calls=%async_computation.15 | async-start | bytes 8388608
  201.1 15.1 %all-to-all-start.7 = ((bf16[32,2,32,128]{3,2,1,0:T(8,128)(2,1)}), bf16[32,2,32,128]{3,2,1,0:T(8,128)(2,1)S(1)}, u32[]{:S(2)}, u32[]{:S(2)}) async-start(bf16[32,2,32,128]{3,2,1,0:T(8,128)(2,1)} %copy.262), calls=%async_computation.7 | async-start | bytes 1048576 | tf_op jit(solution)/shard_map/all_to_all | solution.py:19
  249.7 4.2 %copy-start.3 = (s32[160]{0:T(256)S(1)}, s32[160]{0:T(256)}, u32[]{:S(2)}) copy-start(s32[160]{0:T(256)} %param.9) | copy-start | bytes 1924
  249.7 38.8 %all-to-all-start.8 = ((f32[32,2,8,1280]{3,2,1,0:T(8,128)}), f32[32,2,8,1280]{3,2,1,0:T(8,128)S(1)}, u32[]{:S(2)}, u32[]{:S(2)}) async-start(f32[32,2,8,1280]{3,2,1,0:T(8,128)} %broadcast_in_dim.68), calls=%async_computation.8 | async-start | bytes 5242880 | tf_op jit(solution)/shard_map/all_to_all | solution.py:31
